TPU v7x, 32 devices: a whole 2x2x4 slice. The times are simulated.
32 devices in a mesh: box: 8 (over y, x, core), term: 4 (over z).
Axes of the slice: x: 2, y: 2, z: 4, core: 2. Of those that a mesh axis runs over, the one named last changes fastest.
Arguments:
- fine_coeffs: bfloat16 [4, 64, 32, 1024], P(None, 'box'), may hold values from -6 to 6
- fine_blocks: bfloat16 [16, 3, 32, 32], replicated, may hold values from -0.625 to 0.625
- coarse_blocks: bfloat16 [16, 3, 32, 32], replicated, may hold values from -0.625 to 0.625
- two_scale: bfloat16 [32, 64], replicated, may hold values from -0.75 to 0.75
- term_exponent: int32 [8], replicated, may hold values from 0 to 15
Outputs:
- applied: float32 [4, 64, 32, 1024], P(None, ('box', 'term'))
All inputs are finite; a program needn't handle non-finite values.
Results may differ from a plain program's by a relative error of at most 0.0047.
Values may be sent and summed in bfloat16 or wider, within the bound.
A program may use at most 128 MiB of HBM per device.

v0:
```python
import functools

import jax
import jax.numpy as jnp
from jax import lax
from jax.experimental import pallas as pl
from jax.experimental.pallas import tpu as pltpu
from jax.sharding import PartitionSpec as P

F32 = jnp.float32
BF16 = jnp.bfloat16


def side_count(total):
    return [guess for guess in range(1, 65) if guess * guess * guess == total][0]


def mm(a, b):
    return jnp.dot(a, b, preferred_element_type=F32)


def mm_t(a, b):
    return lax.dot_general(a, b, (((0,), (0,)), ((), ())), preferred_element_type=F32)


def iotas(rows, columns):
    shape = (rows, columns)
    return lax.broadcasted_iota(jnp.int32, shape, 0), lax.broadcasted_iota(jnp.int32, shape, 1)


def ones_where(condition):
    return jnp.where(condition, jnp.float32(1), jnp.float32(0)).astype(BF16)


def build_weights(blocks, exponents, own, terms, k, per, stack, wx, kb, wy):
    ext = own + 2
    tiles = k // per
    lanes = per * k
    row, column = iotas(k, lanes)
    tiled = ones_where(column % k == row)
    row, column = iotas(lanes, lanes)
    same = (row // k) == (column // k)
    for t in range(terms):
        for d in range(3):
            block = blocks[exponents[t], d]
            at = (t * 3 + d) * k
            stack[at : at + k, :] = block
            wide = mm(block, tiled)
            tall = jnp.concatenate([wide] * per, axis=0)
            kb[t, d] = jnp.where(same, tall, 0.0).astype(BF16)
    row, column = iotas(3 * k, ext * k)
    for c in range(own):
        place = ones_where(column == c * k + row)
        for t in range(terms):
            part = stack[t * 3 * k : (t + 1) * 3 * k, :]
            at = (t * own + c) * k
            wx[at : at + k, :] = mm_t(part, place).astype(BF16)
    row, column = iotas(terms * 3 * k, terms * ext * tiles)
    term = row // (3 * k)
    within = row - term * (3 * k)
    target = term * (ext * tiles) + within // per
    for a in range(per):
        for c in range(own):
            place = ones_where((column == target + c * tiles) & (within % per == a))
            at = (a * own + c) * k
            wy[at : at + k, :] = mm_t(stack[...], place).astype(BF16)


def spread_blocks(summed, lane_block, k, per):
    rows = summed.shape[0] // per
    kept = summed[:rows]
    for a in range(1, per):
        kept = jnp.where(lane_block == a, summed[a * rows : (a + 1) * rows], kept)
    shift = k
    while shift < per * k:
        kept = kept + pltpu.roll(kept, shift, 1)
        shift *= 2
    return kept


def sweep(load, own, terms, k, per, wx, kb, wy, a_ref, z_ref, out_ref):
    ext = own + 2
    tiles = k // per
    lanes = per * k
    rows = own * k
    lane_block = lax.broadcasted_iota(jnp.int32, (rows, lanes), 1) // k

    def by_y(yb, carry):
        for zb in range(ext):
            a_ref[zb] = mm(wx[...], load(yb, zb)).astype(BF16)

        def by_term(t, carry):
            parts = []
            for zb in range(ext):
                part = a_ref[zb, pl.ds(pl.multiple_of(t * rows, rows), rows), :]
                parts.append(
                    jnp.concatenate(
                        [part[:, i * lanes : (i + 1) * lanes] for i in range(tiles)], axis=0
                    )
                )
            left = jnp.concatenate(parts, axis=1)
            zero = jnp.zeros((lanes, lanes), BF16)
            right = jnp.concatenate(
                [
                    jnp.concatenate(
                        [kb[t, zb - c] if 0 <= zb - c <= 2 else zero for zb in range(ext)], axis=0
                    )
                    for c in range(own)
                ],
                axis=1,
            )
            result = mm(left, right)
            start = pl.multiple_of((t * ext + yb) * tiles * rows, tiles * rows)
            for c in range(own):
                z_ref[c, pl.ds(start, tiles * rows), :] = result[:, c * lanes : (c + 1) * lanes]
            return carry

        return lax.fori_loop(0, terms, by_term, carry, unroll=2)

    lax.fori_loop(0, ext, by_y, 0)

    def by_u(u, carry):
        right = jnp.concatenate(
            [
                z_ref[c, pl.ds(u, terms * ext * tiles, stride=rows), :].astype(BF16)
                for c in range(own)
            ],
            axis=1,
        )
        result = mm(wy[...], right)
        for c in range(own):
            out_ref[c, pl.ds(pl.multiple_of(u * rows, rows), rows), :] = spread_blocks(
                result[:, c * lanes : (c + 1) * lanes], lane_block, k, per
            )
        return carry

    lax.fori_loop(0, rows, by_u, 0, unroll=4)


def two_parts(value, axis):
    high = value.astype(BF16)
    low = (value - high.astype(F32)).astype(BF16)
    return jnp.concatenate([high, low], axis=axis)


def compute(
    k, per, terms, load_fine, load_coarse, weights, scratch, out_ref, ready=lambda: None
):
    wxf, kbf, wyf, wxc, kbc, wyc, wzu, wtu = weights
    a_f, z_f, out_f, a_c, z_c, out_c, d_ref = scratch
    lanes = per * k
    sweep(load_coarse, 1, terms, k, per, wxc, kbc, wyc, a_c, z_c, out_c)
    lane_block = lax.broadcasted_iota(jnp.int32, (k, lanes), 1) // k

    def unfilter(u, carry):
        value = out_c[0, pl.ds(pl.multiple_of(u * k, k), k), :]
        along_z = mm(two_parts(value, 1), wzu[...])
        along_y = mm(wtu[...], two_parts(along_z, 0))
        for c in range(2):
            d_ref[c, pl.ds(pl.multiple_of(u * 2 * k, 2 * k), 2 * k), :] = along_y[
                :, c * lanes : (c + 1) * lanes
            ]
        return carry

    lax.fori_loop(0, k, unfilter, 0, unroll=8)
    ready()
    sweep(load_fine, 2, terms, k, per, wxf, kbf, wyf, a_f, z_f, out_f)
    wide_block = lax.broadcasted_iota(jnp.int32, (2 * k, lanes), 1) // k
    tiles = k // per
    for cy in range(2):
        for tile in range(tiles):
            for cz in range(2):
                coarse = None
                fine = None
                for a in range(per):
                    v = cy * k + tile * per + a
                    new_c = d_ref[cz, pl.ds(v, k, stride=2 * k), :]
                    new_f = out_f[cz, pl.ds(v, 2 * k, stride=2 * k), :]
                    coarse = new_c if a == 0 else jnp.where(lane_block == a, new_c, coarse)
                    fine = new_f if a == 0 else jnp.where(wide_block == a, new_f, fine)
                total = fine + mm(wtu[...], two_parts(coarse, 0))
                for cx in range(2):
                    out_ref[4 * cx + 2 * cy + cz, :, tile * lanes : (tile + 1) * lanes] = total[
                        cx * k : (cx + 1) * k
                    ].astype(out_ref.dtype)


def kernel(side, k, per, terms, exponents, fine_hbm, coarse_hbm, blocks_f, blocks_c, wzu, wtu, out_ref, *refs):
    scratch = refs[:7]
    x_f, x_c, sem, stack, *built = refs[7:]
    weights = (*built, wzu, wtu)
    count = side * side * side
    me = lax.axis_index("box")
    copies = []

    def shift(i):
        return (i + 1) // 2 - 1

    for yb in range(3):
        for zb in range(3):
            for xb in range(3):
                parent = lax.rem(
                    me + 2 * count + (xb - 1) * side * side + (yb - 1) * side + zb - 1, count
                )
                copies.append(
                    pltpu.make_async_copy(
                        coarse_hbm.at[parent], x_c.at[yb, zb, pl.ds(xb * k, k)], sem.at[0]
                    )
                )
    for yb in range(4):
        for zb in range(4):
            for xb in range(4):
                parent = lax.rem(
                    me + 2 * count + shift(xb) * side * side + shift(yb) * side + shift(zb), count
                )
                child = 4 * ((xb + 1) % 2) + 2 * ((yb + 1) % 2) + (zb + 1) % 2
                copies.append(
                    pltpu.make_async_copy(
                        fine_hbm.at[parent, child], x_f.at[yb, zb, pl.ds(xb * k, k)], sem.at[0]
                    )
                )
    for copy in copies:
        copy.start()
    build_weights(blocks_f, exponents, 2, terms, k, per, stack, *built[:3])
    build_weights(blocks_c, exponents, 1, terms, k, per, stack, *built[3:])
    for copy in copies:
        copy.wait()
    compute(
        k,
        per,
        terms,
        lambda yb, zb: x_f[yb, zb],
        lambda yb, zb: x_c[yb, zb],
        weights,
        scratch,
        out_ref,
    )


def two_scale_weights(scale, k, per):
    lanes = per * k
    row, column = iotas(k, lanes)
    tiled = ones_where(column % k == row)
    row, column = iotas(lanes, lanes)
    same = (row // k) == (column // k)
    spread = mm_t(scale, tiled)
    along_z = jnp.concatenate(
        [
            jnp.where(same, jnp.concatenate([spread[c * k : (c + 1) * k]] * per, axis=0), 0.0)
            for c in range(2)
        ],
        axis=0,
    ).astype(BF16)
    row, column = iotas(2 * k, 2 * k // per)
    along_y = jnp.concatenate(
        [mm(scale, ones_where(row == per * column + a)) for a in range(per)], axis=0
    ).astype(BF16)
    row, column = iotas(2 * k, 2 * lanes)
    once = mm(scale, ones_where(row == (column // lanes) * k + column % k)).astype(BF16)
    padded = jnp.concatenate([once, jnp.zeros(((per - 1) * k, 2 * lanes), BF16)], axis=0)
    back_z = jnp.concatenate([padded, padded], axis=0)
    row, column = iotas(k, 2 * k)
    back = mm_t(scale, ones_where(column % k == row)).astype(BF16)
    return along_z, along_y, back_z, back


def filter_own(own, scale, along_z, along_y, k, per, z_ref, y_ref, out):
    tiles = k // per
    lanes = per * k
    for cx in range(2):
        parts = []
        for cz in range(2):
            pieces = []
            for cy in range(2):
                box = own[4 * cx + 2 * cy + cz]
                pieces += [box[:, i * lanes : (i + 1) * lanes] for i in range(tiles)]
            parts.append(jnp.concatenate(pieces, axis=0))
        result = mm(jnp.concatenate(parts, axis=1), along_z[...])
        z_ref[cx * 2 * tiles * k : (cx + 1) * 2 * tiles * k, :] = result
    lane_block = lax.broadcasted_iota(jnp.int32, (k, lanes), 1) // k

    def by_x(x, carry):
        start = (x // k) * (2 * tiles * k) + x % k
        right = z_ref[pl.ds(start, 2 * tiles, stride=k), :].astype(BF16)
        y_ref[pl.ds(pl.multiple_of(x * k, k), k), :] = spread_blocks(
            mm(along_y[...], right), lane_block, k, per
        )
        return carry

    lax.fori_loop(0, 2 * k, by_x, 0, unroll=8)
    wide_block = lax.broadcasted_iota(jnp.int32, (2 * k, lanes), 1) // k
    for tile in range(tiles):
        picked = y_ref[pl.ds(tile * per, 2 * k, stride=k), :]
        for a in range(1, per):
            other = y_ref[pl.ds(tile * per + a, 2 * k, stride=k), :]
            picked = jnp.where(wide_block == a, other, picked)
        out[:, tile * lanes : (tile + 1) * lanes] = mm(scale[...], picked.astype(BF16)).astype(BF16)


def flip(index, mask):
    y, x, c = index // 4, (index // 2) % 2, index % 2
    y = 1 - y if mask & 4 else y
    x = 1 - x if mask & 2 else x
    c = 1 - c if mask & 1 else c
    return 4 * y + 2 * x + c


FINE_ROUTE = {
    (2, 0): (0, 2), (4, 1): (0, 4), (2, 1): (0, 2), (4, 0): (0, 4), (1, 0): (0, 1), (1, 1): (0, 1),
    (6, 0): (2, 4), (6, 1): (4, 2),
    (3, 0): (2, 1), (3, 1): (2, 1), (5, 0): (4, 1), (5, 1): (4, 1), (7, 0): (6, 1), (7, 1): (6, 1),
}
COARSE_ROUTE = {1: (0, 1), 2: (0, 2), 4: (0, 4), 6: (2, 4), 3: (2, 1), 5: (4, 1), 7: (6, 1)}


def fused_kernel(k, per, terms, groups, exponents, fine, blocks_f, blocks_c, scale, out_ref, *refs):
    scratch = refs[:7]
    all_f, all_c, staged, landed = refs[7:11]
    own_sem, send_f, recv_f, send_c, recv_c, send_o, recv_o = refs[11:18]
    stack, back_z, back, along_z, along_y, filter_z, filter_y = refs[18:25]
    built = refs[25:31]
    me = lax.axis_index("box")
    group = lax.axis_index("term")
    own_copy = pltpu.make_async_copy(fine.at[group], all_f.at[me], own_sem.at[0])
    own_copy.start()
    barrier = pltpu.get_barrier_semaphore()
    for mask in (1, 2, 4):
        pl.semaphore_signal(
            barrier, inc=1, device_id={"box": flip(me, mask)}, device_id_type=pl.DeviceIdType.MESH
        )
    for step in range(1, groups):
        pl.semaphore_signal(
            barrier,
            inc=1,
            device_id={"term": lax.rem(group + step, groups)},
            device_id_type=pl.DeviceIdType.MESH,
        )
    pl.semaphore_wait(barrier, 3 + groups - 1)

    def fine_copy(slot, half, source, target):
        ref = all_f.at[flip(me, source), pl.ds(4 * half, 4)]
        return pltpu.make_async_remote_copy(
            src_ref=ref,
            dst_ref=ref,
            send_sem=send_f.at[slot, half],
            recv_sem=recv_f.at[slot, half],
            device_id={"box": flip(me, target)},
            device_id_type=pl.DeviceIdType.MESH,
        )

    def coarse_copy(slot, source, target):
        ref = all_c.at[flip(me, source)]
        return pltpu.make_async_remote_copy(
            src_ref=ref,
            dst_ref=ref,
            send_sem=send_c.at[slot],
            recv_sem=recv_c.at[slot],
            device_id={"box": flip(me, target)},
            device_id_type=pl.DeviceIdType.MESH,
        )

    def push_fine(*keys):
        for key in keys:
            fine_copy(*key, *FINE_ROUTE[key]).start()

    def arrived_fine(*keys):
        for slot, half in keys:
            fine_copy(slot, half, slot, FINE_ROUTE[slot, half][1]).wait_recv()

    def push_coarse(*keys):
        for key in keys:
            coarse_copy(key, *COARSE_ROUTE[key]).start()

    def arrived_coarse(*keys):
        for slot in keys:
            coarse_copy(slot, slot, COARSE_ROUTE[slot][1]).wait_recv()

    own_copy.wait()
    push_fine((2, 0), (4, 1), (2, 1), (4, 0), (1, 0), (1, 1))
    for ref, value in zip((along_z, along_y, back_z, back), two_scale_weights(scale[...], k, per)):
        ref[...] = value
    filter_own(
        all_f.at[me], scale, along_z, along_y, k, per, filter_z, filter_y, all_c.at[me]
    )
    push_coarse(1, 2, 4)
    arrived_fine((2, 0), (4, 1))
    push_fine((6, 0), (6, 1), (3, 0), (5, 1))
    build_weights(blocks_c, exponents, 1, terms, k, per, stack, *built[3:])
    arrived_coarse(2, 4)
    push_coarse(6, 3, 5)
    arrived_fine((2, 1), (4, 0))
    push_fine((3, 1), (5, 0))
    build_weights(blocks_f, exponents, 2, terms, k, per, stack, *built[:3])
    arrived_coarse(6)
    push_coarse(7)
    arrived_fine((6, 0), (6, 1))
    push_fine((7, 0), (7, 1))
    arrived_coarse(1, 3, 5, 7)

    def all_here():
        arrived_fine(
            (1, 0), (1, 1), (3, 0), (3, 1), (5, 0), (5, 1), (7, 0), (7, 1)
        )

    def load_fine(yb, zb):
        parts = []
        for xb in range(4):
            parent = (
                me + 16 + 4 * ((xb + 1) // 2 - 1) + 2 * ((yb + 1) // 2 - 1) + (zb + 1) // 2 - 1
            ) % 8
            child = 4 * ((xb + 1) % 2) + 2 * ((yb + 1) % 2) + (zb + 1) % 2
            parts.append(all_f[parent, child])
        return jnp.concatenate(parts, axis=0)

    def load_coarse(yb, zb):
        parts = [
            all_c[(me + 16 + 4 * (xb - 1) + 2 * (yb - 1) + zb - 1) % 8] for xb in range(3)
        ]
        return jnp.concatenate(parts, axis=0)

    compute(
        k, per, terms, load_fine, load_coarse, (*built, back_z, back), scratch, staged, all_here
    )
    pushes = []
    share = 8 // groups
    for step in range(1, groups):
        target = lax.rem(group + step, groups)
        copy = pltpu.make_async_remote_copy(
            src_ref=staged.at[pl.ds(target * share, share)],
            dst_ref=landed.at[group],
            send_sem=send_o.at[step],
            recv_sem=recv_o.at[step],
            device_id={"term": target},
            device_id_type=pl.DeviceIdType.MESH,
        )
        copy.start()
        pushes.append(copy)
    out_ref[group] = staged[pl.ds(group * share, share)]
    for key, (source, target) in FINE_ROUTE.items():
        fine_copy(*key, source, target).wait_send()
    for key, (source, target) in COARSE_ROUTE.items():
        coarse_copy(key, source, target).wait_send()
    for step in range(1, groups):
        pushes[step - 1].wait()
        origin = lax.rem(group + groups - step, groups)
        out_ref[origin] = landed[origin]


def fused(fine_coeffs, fine_blocks, coarse_blocks, two_scale, exponents, per):
    k = two_scale.shape[0]
    terms = exponents.shape[0]
    groups = lax.axis_size("term")
    tiles = k // per
    lanes = per * k
    vmem = pl.BlockSpec(memory_space=pltpu.VMEM)
    dma = pltpu.SemaphoreType.DMA
    return pl.pallas_call(
        functools.partial(fused_kernel, k, per, terms, groups),
        out_shape=jax.ShapeDtypeStruct((groups, 8 // groups, k, k * k), BF16),
        in_specs=[pl.BlockSpec(memory_space=pltpu.SMEM), pl.BlockSpec(memory_space=pl.ANY)] + [vmem] * 3,
        out_specs=vmem,
        scratch_shapes=pass_scratch(terms, k, per)
        + [
            pltpu.VMEM((8, 8, k, k * k), BF16),
            pltpu.VMEM((8, k, k * k), BF16),
            pltpu.VMEM((8, k, k * k), BF16),
            pltpu.VMEM((groups, 8 // groups, k, k * k), BF16),
            dma((1,)),
            dma((8, 2)),
            dma((8, 2)),
            dma((8,)),
            dma((8,)),
            dma((groups,)),
            dma((groups,)),
            pltpu.VMEM((terms * 3 * k, k), BF16),
            pltpu.VMEM((2 * lanes, 2 * lanes), BF16),
            pltpu.VMEM((2 * k, 2 * k), BF16),
            pltpu.VMEM((2 * lanes, lanes), BF16),
            pltpu.VMEM((lanes, 2 * tiles), BF16),
            pltpu.VMEM((2 * 2 * tiles * k, lanes), F32),
            pltpu.VMEM((2 * k * k, lanes), F32),
        ]
        + weight_scratch(terms, k, per),
        compiler_params=pltpu.CompilerParams(
            vmem_limit_bytes=58 * 1024 * 1024, collective_id=0, has_side_effects=True
        ),
    )(exponents, fine_coeffs, fine_blocks, coarse_blocks, two_scale)


def pass_scratch(terms, k, per):
    tiles = k // per
    return [
        pltpu.VMEM((4, terms * 2 * k, k * k), BF16),
        pltpu.VMEM((2, terms * 4 * tiles * 2 * k, per * k), F32),
        pltpu.VMEM((2, 4 * k * k, per * k), F32),
        pltpu.VMEM((3, terms * k, k * k), BF16),
        pltpu.VMEM((1, terms * 3 * tiles * k, per * k), F32),
        pltpu.VMEM((1, k * k, per * k), F32),
        pltpu.VMEM((2, 2 * k * k, per * k), F32),
    ]


def weight_scratch(terms, k, per):
    tiles = k // per
    return [
        pltpu.VMEM((terms * 2 * k, 4 * k), BF16),
        pltpu.VMEM((terms, 3, per * k, per * k), BF16),
        pltpu.VMEM((per * 2 * k, terms * 4 * tiles), BF16),
        pltpu.VMEM((terms * k, 3 * k), BF16),
        pltpu.VMEM((terms, 3, per * k, per * k), BF16),
        pltpu.VMEM((per * k, terms * 3 * tiles), BF16),
    ]


def unfilter_weights(two_scale, per):
    k = two_scale.shape[0]
    once = jnp.repeat(two_scale.reshape(k, 2, 1, k), per, axis=2).reshape(k, 2 * per * k)
    once = jnp.pad(once, ((0, (per - 1) * k), (0, 0)))
    wzu = jnp.concatenate([once, once], axis=0)
    wtu = jnp.concatenate([two_scale.T, two_scale.T], axis=1)
    return wzu, wtu


def filtered(chosen, two_scale):
    k = two_scale.shape[0]
    cells = chosen.reshape(2, 2, 2, k, k, k)
    scale = two_scale.reshape(k, 2, k)
    parent = jnp.einsum("xyzabe,kze->xyabk", cells, scale, preferred_element_type=F32).astype(BF16)
    parent = jnp.einsum("xyabk,jyb->xajk", parent, scale, preferred_element_type=F32).astype(BF16)
    parent = jnp.einsum("xajk,ixa->ijk", parent, scale, preferred_element_type=F32).astype(BF16)
    return parent.reshape(k, k * k)


def on_device(fine_coeffs, fine_blocks, coarse_blocks, two_scale, term_exponent):
    count = lax.axis_size("box")
    side = side_count(count)
    k = two_scale.shape[0]
    terms = term_exponent.shape[0]
    per = 128 // k
    groups = lax.axis_size("term")
    own = fine_coeffs.shape[0] // groups
    if side == 2 and own == 1 and 8 % groups == 0:
        return fused(
            fine_coeffs, fine_blocks, coarse_blocks, two_scale, term_exponent, per
        ).astype(F32)
    chosen = lax.dynamic_slice_in_dim(fine_coeffs, lax.axis_index("term") * own, own, 0)
    weights = unfilter_weights(two_scale, per)
    any_space = pl.BlockSpec(memory_space=pl.ANY)
    vmem = pl.BlockSpec(memory_space=pltpu.VMEM)
    tiles = k // per
    results = []
    for f in range(own):
        parent = filtered(chosen[f], two_scale)
        fine_all = lax.all_gather(chosen[f], "box")
        coarse_all = lax.all_gather(parent, "box")
        results.append(
            pl.pallas_call(
                functools.partial(kernel, side, k, per, terms),
                out_shape=jax.ShapeDtypeStruct((8, k, k * k), BF16),
                in_specs=[pl.BlockSpec(memory_space=pltpu.SMEM), any_space, any_space] + [vmem] * 4,
                out_specs=vmem,
                scratch_shapes=pass_scratch(terms, k, per)
                + [
                    pltpu.VMEM((4, 4, 4 * k, k * k), BF16),
                    pltpu.VMEM((3, 3, 3 * k, k * k), BF16),
                    pltpu.SemaphoreType.DMA((1,)),
                    pltpu.VMEM((terms * 3 * k, k), BF16),
                ]
                + weight_scratch(terms, k, per),
                compiler_params=pltpu.CompilerParams(vmem_limit_bytes=58 * 1024 * 1024),
            )(term_exponent, fine_all, coarse_all, fine_blocks, coarse_blocks, *weights)
        )
    box_rows = jnp.stack(results)
    return lax.all_to_all(box_rows, "term", split_axis=1, concat_axis=0, tiled=True).astype(F32)


def solution(mesh):
    placed = (P(None, "box", None, None), P(), P(), P(), P())
    return jax.shard_map(
        on_device,
        mesh=mesh,
        in_specs=placed,
        out_specs=P(None, ("box", "term"), None, None),
        check_vma=False,
    )
```

profile of v0, /device:TPU:9, one launch (start us, length us, event | category | flops | bytes accessed | tf_op | source)
XLA Modules:
  0.0 87.9 jit_solution(5987088297920280341)
XLA Ops:
  0.0 85.8 %shard_map.55 = bf16[4,2,32,1024]{3,2,1,0:T(8,128)(2,1)} custom-call(s32[8]{0:T(128)} %exponents.1, bf16[4,8,32,1024]{3,2,1,0:T(8,128)(2,1)} %fine.1, bf16[16,3,32,32]{3,2,1,0:T(8,128)(2,1)} %blocks_f.1, bf16[16,3,32,32]{3,2,1,0:T(8,128)(2,1)} %blocks_c.1, bf16[32,64]{1,0:T(8,128)(2,1)} %scale.1), custom_call_target="tpu_custom_call" | custom-call | tf_op jit(solution)/shard_map/pallas_call | solution.py:457
  85.8 2.1 %convert_element_type.3 = f32[4,2,32,1024]{3,2,1,0:T(8,128)} convert(bf16[4,2,32,1024]{3,2,1,0:T(8,128)(2,1)} %shard_map.55) | non-fusion elementwise | flops 262144 | bytes 1572864 | tf_op jit(solution)/shard_map/convert_element_type | solution.py:545
where the time goes:
time: 88.1 us; the launch traced here: 87.9 us
  Pallas kernels  85.8 us (97%)
  other arithmetic  2.13 us (2%)
    pallas_call x1, Pallas kernels, fused(): pl.pallas_call(functools.partial(fused_kernel, k, per, terms, groups), ou...  85.8 us
    convert_element_type x1, other arithmetic, on_device(): return fused(fine_coeffs, fine_blocks, coarse_blocks, two_scale, term_exp...  2.13 us

commit v1 on v0

--- a/solution.py
+++ b/solution.py
@@ -115,7 +115,7 @@
                 z_ref[c, pl.ds(start, tiles * rows), :] = result[:, c * lanes : (c + 1) * lanes]
             return carry
 
-        return lax.fori_loop(0, terms, by_term, carry, unroll=2)
+        return lax.fori_loop(0, terms, by_term, carry, unroll=4)
 
     lax.fori_loop(0, ext, by_y, 0)
 
@@ -134,7 +134,7 @@
             )
         return carry
 
-    lax.fori_loop(0, rows, by_u, 0, unroll=4)
+    lax.fori_loop(0, rows, by_u, 0, unroll=8)
 
 
 def two_parts(value, axis):
@@ -144,12 +144,14 @@
 
 
 def compute(
-    k, per, terms, load_fine, load_coarse, weights, scratch, out_ref, ready=lambda: None
+    k, per, terms, load_fine, load_coarse, weights, scratch, out_ref, relay=lambda: None, ready=lambda: None,
+    done=lambda cy: None,
 ):
     wxf, kbf, wyf, wxc, kbc, wyc, wzu, wtu = weights
     a_f, z_f, out_f, a_c, z_c, out_c, d_ref = scratch
     lanes = per * k
     sweep(load_coarse, 1, terms, k, per, wxc, kbc, wyc, a_c, z_c, out_c)
+    relay()
     lane_block = lax.broadcasted_iota(jnp.int32, (k, lanes), 1) // k
 
     def unfilter(u, carry):
@@ -183,6 +185,7 @@
                     out_ref[4 * cx + 2 * cy + cz, :, tile * lanes : (tile + 1) * lanes] = total[
                         cx * k : (cx + 1) * k
                     ].astype(out_ref.dtype)
+        done(cy)
 
 
 def kernel(side, k, per, terms, exponents, fine_hbm, coarse_hbm, blocks_f, blocks_c, wzu, wtu, out_ref, *refs):
@@ -393,9 +396,11 @@
     build_weights(blocks_f, exponents, 2, terms, k, per, stack, *built[:3])
     arrived_coarse(6)
     push_coarse(7)
-    arrived_fine((6, 0), (6, 1))
-    push_fine((7, 0), (7, 1))
     arrived_coarse(1, 3, 5, 7)
+
+    def relay_last():
+        arrived_fine((6, 0), (6, 1))
+        push_fine((7, 0), (7, 1))
 
     def all_here():
         arrived_fine(
@@ -418,14 +423,11 @@
         ]
         return jnp.concatenate(parts, axis=0)
 
-    compute(
-        k, per, terms, load_fine, load_coarse, (*built, back_z, back), scratch, staged, all_here
-    )
-    pushes = []
     share = 8 // groups
-    for step in range(1, groups):
-        target = lax.rem(group + step, groups)
-        copy = pltpu.make_async_remote_copy(
+
+    def push_result(target):
+        step = lax.rem(target - group + groups, groups)
+        return pltpu.make_async_remote_copy(
             src_ref=staged.at[pl.ds(target * share, share)],
             dst_ref=landed.at[group],
             send_sem=send_o.at[step],
@@ -433,15 +435,23 @@
             device_id={"term": target},
             device_id_type=pl.DeviceIdType.MESH,
         )
-        copy.start()
-        pushes.append(copy)
+
+    def done(cy):
+        ready = [cy, 2 + cy] if share == 2 else range(groups * cy)
+        for target in ready:
+            pl.when(group != target)(lambda target=target: push_result(target).start())
+
+    compute(
+        k, per, terms, load_fine, load_coarse, (*built, back_z, back), scratch, staged,
+        relay_last, all_here, done,
+    )
     out_ref[group] = staged[pl.ds(group * share, share)]
     for key, (source, target) in FINE_ROUTE.items():
         fine_copy(*key, source, target).wait_send()
     for key, (source, target) in COARSE_ROUTE.items():
         coarse_copy(key, source, target).wait_send()
     for step in range(1, groups):
-        pushes[step - 1].wait()
+        push_result(lax.rem(group + step, groups)).wait()
         origin = lax.rem(group + groups - step, groups)
         out_ref[origin] = landed[origin]
 

time: 88.1 us -> 80 us (0.908)
  Pallas kernels: 85.8 us -> 77.7 us
    pallas_call x1, Pallas kernels: 85.8 us -> 77.7 us  [fused(): pl.pallas_call(functools.partial(fused_kernel, k, per, terms, groups), ou...]
where the time goes in v1:
time: 80 us; the launch traced here: 79.8 us
  Pallas kernels  77.7 us (97%)
  other arithmetic  2.13 us (3%)
    pallas_call x1, Pallas kernels, fused(): pl.pallas_call(functools.partial(fused_kernel, k, per, terms, groups), ou...  77.7 us
    convert_element_type x1, other arithmetic, on_device(): return fused(fine_coeffs, fine_blocks, coarse_blocks, two_scale, term_exp...  2.13 us

profile of v1, /device:TPU:9, one launch (start us, length us, event | category | flops | bytes accessed | tf_op | source)
XLA Modules:
  0.0 79.8 jit_solution(3670351606909557726)
XLA Ops:
  0.0 77.7 %shard_map.55 = bf16[4,2,32,1024]{3,2,1,0:T(8,128)(2,1)} custom-call(s32[8]{0:T(128)} %exponents.1, bf16[4,8,32,1024]{3,2,1,0:T(8,128)(2,1)} %fine.1, bf16[16,3,32,32]{3,2,1,0:T(8,128)(2,1)} %blocks_f.1, bf16[16,3,32,32]{3,2,1,0:T(8,128)(2,1)} %blocks_c.1, bf16[32,64]{1,0:T(8,128)(2,1)} %scale.1), custom_call_target="tpu_custom_call" | custom-call | tf_op jit(solution)/shard_map/pallas_call | solution.py:467
  77.7 2.1 %convert_element_type.3 = f32[4,2,32,1024]{3,2,1,0:T(8,128)} convert(bf16[4,2,32,1024]{3,2,1,0:T(8,128)(2,1)} %shard_map.55) | non-fusion elementwise | flops 262144 | bytes 1572864 | tf_op jit(solution)/shard_map/convert_element_type | solution.py:555
